TPU v7x, 256 devices: a whole 4x4x8 slice. The times are simulated.
256 devices in a mesh: seq: 128 (over z, x, y), hid: 2 (over core).
Axes of the slice: x: 4, y: 4, z: 8, core: 2. Of those that a mesh axis runs over, the one named last changes fastest.
Arguments:
- tokens: bfloat16 [16384, 768], P('seq', 'hid'), may hold values from -6 to 6
- norm_gain: float32 [768], P('hid'), may hold values from 0.5 to 2
- in_weight: bfloat16 [3, 768, 768], P(None, None, 'hid'), may hold values from -0.21875 to 0.21875
- short_filter: float32 [3, 3, 768], P(None, None, 'hid'), may hold values from -1 to 1
- spectrum: float32 [2, 16384, 768], P(None, 'seq', 'hid'), may hold values from -6 to 6
- out_weight: bfloat16 [768, 768], P('hid'), may hold values from -0.21875 to 0.21875
- mlp_gain: float32 [768], P('hid'), may hold values from 0.4 to 2.3
- up_weight: bfloat16 [768, 3072], P(None, 'hid'), may hold values from -0.21650635 to 0.21650635
- down_weight: bfloat16 [768, 3072], P(None, 'hid'), may hold values from -0.15155445 to 0.15155445
- cotangent: bfloat16 [16384, 768], P('seq', 'hid'), may hold values from -6 to 6
Outputs:
- output: bfloat16 [16384, 768], P('seq', 'hid')
- grad_tokens: bfloat16 [16384, 768], P('seq', 'hid')
- grad_up: float32 [768, 3072], P('seq', 'hid')
- grad_down: float32 [768, 3072], P('seq', 'hid')
All inputs are finite; a program needn't handle non-finite values.
Results may differ from a plain program's by a relative error of at most 0.0095.
Values may be sent and summed in bfloat16 or wider, within the bound.
A program may use at most 128 MiB of HBM per device.

v0:
```python
import math

import jax
import jax.numpy as jnp
from jax import lax
from jax.sharding import PartitionSpec as P

EPSILON = 1e-05
GELU_SCALE = 0.7978845608028654
PRECISE = lax.Precision.HIGHEST


def partner_2(value, axis, stride):
    mask = 2**stride
    pairs = [(source, source ^ mask) for source in range(lax.axis_size(axis))]
    return lax.ppermute(value, axis, pairs)


def passed_along(value, axis, steps):
    count = lax.axis_size(axis)
    leading, last = (max(0, -steps), min(count, count - steps))
    return lax.ppermute(value, axis, [(source, source + steps) for source in range(leading, last)])


def gelu_value(values):
    inner = GELU_SCALE * (values + 0.044715 * values * values * values)
    return 0.5 * values * (1.0 + jnp.tanh(inner))


def gelu_slope(values):
    tanh_val = jnp.tanh(GELU_SCALE * (values + 0.044715 * values * values * values))
    return 0.5 * (1.0 + tanh_val) + 0.5 * values * (1.0 - tanh_val * tanh_val) * GELU_SCALE * (
        1.0 + 3.0 * 0.044715 * values * values
    )


def reversed_bits(position, bit_count):
    result = jnp.zeros_like(position)
    for place in range(bit_count):
        result = result + (position >> place & 1) * (1 << bit_count - 1 - place)
    return result


def turn(numer, denom):
    return 2.0 * math.pi / denom * (numer % denom).astype(jnp.float32)


def precise_dot(left, right):
    return jnp.dot(left, right, precision=PRECISE, preferred_element_type=jnp.float32)


def complex_apply(cosine, sine, direction, complex_parts):
    real_part = precise_dot(cosine, complex_parts[0]) - direction * precise_dot(
        sine, complex_parts[1]
    )
    imag_part = precise_dot(cosine, complex_parts[1]) + direction * precise_dot(
        sine, complex_parts[0]
    )
    return jnp.stack([real_part, imag_part])


def forward_tail(complex_parts, first_freq, length_all):
    row_count = complex_parts.shape[1]
    positions = lax.iota(jnp.int32, row_count)
    angles = turn(positions * first_freq, length_all)[:, None]
    cosine = jnp.cos(angles)
    sine = jnp.sin(angles)
    twisted = jnp.stack(
        [
            complex_parts[0] * cosine + complex_parts[1] * sine,
            complex_parts[1] * cosine - complex_parts[0] * sine,
        ]
    )
    table = turn(positions[:, None] * positions[None, :], row_count)
    return complex_apply(jnp.cos(table), jnp.sin(table), -1.0, twisted)


def forward_transform(signal):
    row_count, chan_count = signal.shape
    splits = lax.axis_size("seq")
    bit_count = splits.bit_length() - 1
    own_index = lax.axis_index("seq")
    length_all = row_count * splits
    first_freq = reversed_bits(own_index, bit_count)
    top_bit = bit_count - 1
    half_span = 1 << top_bit
    partner = partner_2(signal, "seq", top_bit)
    upper_half = own_index >> top_bit & 1 == 1
    angle = turn(own_index % half_span, 2 * half_span)
    difference = partner - signal
    real_part = jnp.where(upper_half, difference * jnp.cos(angle), signal + partner)
    imag_part = jnp.where(upper_half, -difference * jnp.sin(angle), jnp.zeros_like(signal))
    current = jnp.stack([real_part, imag_part])
    for section_bit in range(bit_count - 2, -1, -1):
        half_span = 1 << section_bit
        partner = partner_2(current, "seq", section_bit)
        upper_half = own_index >> section_bit & 1 == 1
        angle = turn(own_index % half_span, 2 * half_span)
        cosine = jnp.cos(angle)
        sine = jnp.sin(angle)
        difference = partner - current
        rotated = jnp.stack(
            [
                difference[0] * cosine + difference[1] * sine,
                difference[1] * cosine - difference[0] * sine,
            ]
        )
        current = jnp.where(upper_half, rotated, current + partner)
    return forward_tail(current, first_freq, length_all)


def inverse_transform(complex_parts):
    row_count = complex_parts.shape[1]
    chan_count = complex_parts.shape[2]
    splits = lax.axis_size("seq")
    bit_count = splits.bit_length() - 1
    own_index = lax.axis_index("seq")
    length_all = row_count * splits
    share = row_count // splits
    positions = lax.iota(jnp.int32, row_count)
    table = turn(positions[:, None] * positions[None, :], row_count)
    spatial = complex_apply(jnp.cos(table), jnp.sin(table), 1.0, complex_parts)
    first_freq = reversed_bits(own_index, bit_count)
    angles = turn(positions * first_freq, length_all)[:, None]
    cosine = jnp.cos(angles)
    sine = jnp.sin(angles)
    twisted = jnp.stack(
        [spatial[0] * cosine - spatial[1] * sine, spatial[1] * cosine + spatial[0] * sine]
    )
    gathered = lax.all_to_all(
        twisted.reshape(2, 1, row_count, chan_count), "seq", split_axis=2, concat_axis=1, tiled=True
    )
    flat = gathered.reshape(2, splits, share * chan_count)
    sources = lax.iota(jnp.int32, splits)
    phase = turn(sources[:, None] * reversed_bits(sources, bit_count)[None, :], splits)
    real_out = (precise_dot(jnp.cos(phase), flat[0]) - precise_dot(jnp.sin(phase), flat[1])) * (
        1.0 / length_all
    )
    return lax.all_to_all(real_out, "seq", split_axis=0, concat_axis=0, tiled=True)


def times_spectrum(complex_parts, spectrum, direction):
    real_part = spectrum[0] * complex_parts[0] - direction * spectrum[1] * complex_parts[1]
    imag_part = spectrum[0] * complex_parts[1] + direction * spectrum[1] * complex_parts[0]
    return jnp.stack([real_part, imag_part])


def local(
    tokens,
    norm_gain,
    in_weight,
    short_filter,
    spectrum,
    out_weight,
    mlp_gain,
    up_weight,
    down_weight,
    cotangent,
):
    row_count, chan_count = tokens.shape
    model_width = in_weight.shape[1]
    hid_units = up_weight.shape[1]
    tap_count = short_filter.shape[1]
    splits = lax.axis_size("seq")
    tokens_f = tokens.astype(jnp.float32)
    squares_in = lax.psum(jnp.sum(tokens_f * tokens_f, axis=1), "hid")
    scale_in = lax.rsqrt(squares_in / model_width + EPSILON)
    normed_in = tokens_f * scale_in[:, None]
    inputs_b = (normed_in * norm_gain[None, :]).astype(jnp.bfloat16)
    weight_block = in_weight
    projected = jnp.einsum(
        "td,jdc->jtc",
        lax.all_gather(inputs_b, "hid", axis=1, tiled=True),
        weight_block,
        preferred_element_type=jnp.float32,
    )
    rim_before = passed_along(projected[:, row_count - (tap_count - 1) :, :], "seq", 1)
    extended = jnp.concatenate([rim_before, projected], axis=1)
    shorted = jnp.zeros_like(projected)
    for tap_index in range(tap_count):
        begin = tap_count - 1 - tap_index
        shorted = (
            shorted
            + short_filter[:, tap_index, None, :] * extended[:, begin : begin + row_count, :]
        )
    signal = shorted[1] * shorted[0]
    conv = inverse_transform(times_spectrum(forward_transform(signal), spectrum, 1.0))
    mixed_y = (shorted[2] * conv).astype(jnp.bfloat16)
    mix_terms = jnp.dot(mixed_y, out_weight, preferred_element_type=jnp.float32)
    resid_one = tokens_f + lax.psum_scatter(mix_terms, "hid", scatter_dimension=1, tiled=True)
    squares_two = lax.psum(jnp.sum(resid_one * resid_one, axis=1), "hid")
    scale_two = lax.rsqrt(squares_two / model_width + EPSILON)
    normed_two = resid_one * scale_two[:, None]
    mlp_local = (normed_two * mlp_gain[None, :]).astype(jnp.bfloat16)
    mlp_full = lax.all_gather(mlp_local, "hid", axis=1, tiled=True)
    pre = jnp.dot(mlp_full, up_weight, preferred_element_type=jnp.float32)
    hidden = gelu_value(pre).astype(jnp.bfloat16)
    last_dims = (((1,), (1,)), ((), ()))
    down_terms = lax.dot_general(hidden, down_weight, last_dims, preferred_element_type=jnp.float32)
    output = (
        resid_one + lax.psum_scatter(down_terms, "hid", scatter_dimension=1, tiled=True)
    ).astype(jnp.bfloat16)
    cot_full = lax.all_gather(cotangent, "hid", axis=1, tiled=True)
    d_hidden = jnp.dot(cot_full, down_weight, preferred_element_type=jnp.float32)
    d_pre = (d_hidden * gelu_slope(pre)).astype(jnp.bfloat16)
    first_dims = (((0,), (0,)), ((), ()))
    up_part = lax.dot_general(mlp_full, d_pre, first_dims, preferred_element_type=jnp.float32)
    down_part = lax.dot_general(cot_full, hidden, first_dims, preferred_element_type=jnp.float32)
    summed = lax.psum_scatter(
        jnp.concatenate([up_part, down_part], axis=1), "seq", scatter_dimension=0, tiled=True
    )
    grad_scale = 1.0 / math.sqrt(row_count * splits)
    grad_up = summed[:, :hid_units] * grad_scale
    grad_down = summed[:, hid_units:] * grad_scale
    back_terms = lax.dot_general(d_pre, up_weight, last_dims, preferred_element_type=jnp.float32)
    d_n2 = lax.psum_scatter(back_terms, "hid", scatter_dimension=1, tiled=True) * mlp_gain[None, :]
    inner_two = lax.psum(jnp.sum(d_n2 * normed_two, axis=1), "hid") / model_width
    d_resid = cotangent.astype(jnp.float32) + scale_two[:, None] * (
        d_n2 - normed_two * inner_two[:, None]
    )
    d_resid_b = d_resid.astype(jnp.bfloat16)
    weight_block = out_weight
    d_mixed = lax.dot_general(
        lax.all_gather(d_resid_b, "hid", axis=1, tiled=True),
        weight_block,
        last_dims,
        preferred_element_type=jnp.float32,
    )
    d_conv = d_mixed * shorted[2]
    d_outer = d_mixed * conv
    d_signal = inverse_transform(times_spectrum(forward_transform(d_conv), spectrum, -1.0))
    d_short = jnp.stack([d_signal * shorted[1], d_signal * shorted[0], d_outer])
    rim_after = passed_along(d_short[:, : tap_count - 1, :], "seq", -1)
    extended_back = jnp.concatenate([d_short, rim_after], axis=1)
    d_proj = jnp.zeros_like(d_short)
    for tap_index in range(tap_count):
        d_proj = (
            d_proj
            + short_filter[:, tap_index, None, :]
            * extended_back[:, tap_index : tap_index + row_count, :]
        )
    d_proj = d_proj.astype(jnp.bfloat16)
    input_terms = jnp.einsum("jtc,jdc->td", d_proj, in_weight, preferred_element_type=jnp.float32)
    d_n1 = (
        lax.psum_scatter(input_terms, "hid", scatter_dimension=1, tiled=True) * norm_gain[None, :]
    )
    inner_one = lax.psum(jnp.sum(d_n1 * normed_in, axis=1), "hid") / model_width
    grad_tokens = (d_resid + scale_in[:, None] * (d_n1 - normed_in * inner_one[:, None])).astype(
        jnp.bfloat16
    )
    return (output, grad_tokens, grad_up, grad_down)


def solution(mesh):
    return jax.shard_map(
        local,
        mesh=mesh,
        in_specs=(
            P("seq", "hid"),
            P("hid"),
            P(None, None, "hid"),
            P(None, None, "hid"),
            P(None, "seq", "hid"),
            P("hid", None),
            P("hid"),
            P(None, "hid"),
            P(None, "hid"),
            P("seq", "hid"),
        ),
        out_specs=(P("seq", "hid"), P("seq", "hid"), P("seq", "hid"), P("seq", "hid")),
        check_vma=False,
    )
```

profile of v0, /device:TPU:1, one launch (start us, length us, event | category | flops | bytes accessed | tf_op | source)
XLA Modules:
  0.0 683.9 jit_solution(18077843635028830272)
XLA Ops:
  21.1 12.8 %collective-permute-start.1 = (f32[128,384]{1,0:T(8,128)S(1)}, f32[128,384]{1,0:T(8,128)S(1)}, u32[]{:S(2)}, u32[]{:S(2)}) collective-permute-start(f32[128,384]{1,0:T(8,128)S(1)} %multiply_bitcast_fusion), channel_id=1, source_target_pairs={{0,128},{2,130},{4,132},{6,134},{8,136},{10,138},{12,140},{14,142}... | collective-permute-start | bytes 589832 | tf_op jit(solution)/shard_map/ppermute | solution.py:16
  41.7 16.4 %collective-permute-done.2 = f32[2,128,384]{2,1,0:T(8,128)} collective-permute-done((f32[2,128,384]{2,1,0:T(8,128)}, f32[2,128,384]{2,1,0:T(8,128)}, u32[]{:S(2)}, u32[]{:S(2)}) %collective-permute-start.2) | collective-permute-done | bytes 393248 | tf_op jit(solution)/shard_map/ppermute | solution.py:16
  62.0 8.5 %collective-permute-done.3 = f32[2,128,384]{2,1,0:T(8,128)} collective-permute-done((f32[2,128,384]{2,1,0:T(8,128)}, f32[2,128,384]{2,1,0:T(8,128)}, u32[]{:S(2)}, u32[]{:S(2)}) %collective-permute-start.3) | collective-permute-done | bytes 393248 | tf_op jit(solution)/shard_map/ppermute | solution.py:16
  79.8 8.1 %collective-permute-done.4 = f32[2,128,384]{2,1,0:T(8,128)S(1)} collective-permute-done((f32[2,128,384]{2,1,0:T(8,128)}, f32[2,128,384]{2,1,0:T(8,128)S(1)}, u32[]{:S(2)}, u32[]{:S(2)}) %collective-permute-start.4) | collective-permute-done | bytes 393248 | tf_op jit(solution)/shard_map/ppermute | solution.py:16
  91.8 7.4 %collective-permute-done.5 = f32[2,128,384]{2,1,0:T(8,128)} collective-permute-done((f32[2,128,384]{2,1,0:T(8,128)S(1)}, f32[2,128,384]{2,1,0:T(8,128)}, u32[]{:S(2)}, u32[]{:S(2)}) %collective-permute-start.5) | collective-permute-done | bytes 393248 | tf_op jit(solution)/shard_map/ppermute | solution.py:16
  102.3 8.7 %collective-permute-done.6 = f32[2,128,384]{2,1,0:T(8,128)} collective-permute-done((f32[2,128,384]{2,1,0:T(8,128)S(1)}, f32[2,128,384]{2,1,0:T(8,128)}, u32[]{:S(2)}, u32[]{:S(2)}) %collective-permute-start.6) | collective-permute-done | bytes 393248 | tf_op jit(solution)/shard_map/ppermute | solution.py:16
  114.0 6.8 collective-permute-done.7
  128.9 12.2 %all-to-all-start = ((f32[2,1,128,384]{3,0,1,2:T(2,128)}), f32[2,1,128,384]{3,0,1,2:T(2,128)}, u32[]{:S(2)}, u32[]{:S(2)}) async-start(f32[2,1,128,384]{3,0,1,2:T(2,128)} %copy.16), calls=%async_computation | async-start | bytes 786432 | tf_op jit(solution)/shard_map/all_to_all | solution.py:130
  141.2 13.6 %all-to-all-done = f32[2,1,128,384]{3,0,1,2:T(2,128)} async-done(((f32[2,1,128,384]{3,0,1,2:T(2,128)}), f32[2,1,128,384]{3,0,1,2:T(2,128)}, u32[]{:S(2)}, u32[]{:S(2)}) %all-to-all-start) | async-done | bytes 393248 | tf_op jit(solution)/shard_map/all_to_all | solution.py:130
  157.7 17.4 %all_to_all.42 = f32[128,1,384]{2,1,0:T(1,128)S(1)} all-to-all(f32[128,1,384]{2,1,0:T(1,128)S(1)} %copy.17), channel_id=1, replica_groups=mesh['seq'=128,'hid'=2] {'seq'}, dimensions={0} | all-to-all | bytes 393216 | tf_op jit(solution)/shard_map/all_to_all | solution.py:139
  176.9 9.3 %all_gather.14 = bf16[128,768]{1,0:T(8,128)(2,1)S(1)} all-gather(bf16[128,384]{1,0:T(8,128)(2,1)S(1)} %copy-done.15), channel_id=1, replica_groups=mesh['seq'=128,'hid'=2] {'hid'}, dimensions={1}, use_global_device_ids=true | all-gather | bytes 294912 | tf_op jit(solution)/shard_map/all_gather | solution.py:203
  202.5 14.5 %reduce-scatter.9.cloned.1.call-done = f32[128,384]{1,0:T(8,128)} async-done(((f32[128,768]{1,0:T(8,128)}), f32[128,384]{1,0:T(8,128)}) %reduce-scatter.9.cloned.1.call-update) | async-done | bytes 196624 | tf_op jit(solution)/shard_map/reduce_scatter | solution.py:216
  230.3 6.8 collective-permute-done.8
  242.1 17.3 %collective-permute-done.9 = f32[2,128,384]{2,1,0:T(8,128)S(1)} collective-permute-done((f32[2,128,384]{2,1,0:T(8,128)S(1)}, f32[2,128,384]{2,1,0:T(8,128)S(1)}, u32[]{:S(2)}, u32[]{:S(2)}) %collective-permute-start.9) | collective-permute-done | bytes 393248 | tf_op jit(solution)/shard_map/ppermute | solution.py:16
  259.7 10.2 %collective-permute-done.10 = f32[2,128,384]{2,1,0:T(8,128)S(1)} collective-permute-done((f32[2,128,384]{2,1,0:T(8,128)S(1)}, f32[2,128,384]{2,1,0:T(8,128)S(1)}, u32[]{:S(2)}, u32[]{:S(2)}) %collective-permute-start.10) | collective-permute-done | bytes 393248 | tf_op jit(solution)/shard_map/ppermute | solution.py:16
  272.9 8.1 %collective-permute-done.11 = f32[2,128,384]{2,1,0:T(8,128)S(1)} collective-permute-done((f32[2,128,384]{2,1,0:T(8,128)S(1)}, f32[2,128,384]{2,1,0:T(8,128)S(1)}, u32[]{:S(2)}, u32[]{:S(2)}) %collective-permute-start.11) | collective-permute-done | bytes 393248 | tf_op jit(solution)/shard_map/ppermute | solution.py:16
  282.4 7.2 %collective-permute-done.12 = f32[2,128,384]{2,1,0:T(8,128)S(1)} collective-permute-done((f32[2,128,384]{2,1,0:T(8,128)S(1)}, f32[2,128,384]{2,1,0:T(8,128)S(1)}, u32[]{:S(2)}, u32[]{:S(2)}) %collective-permute-start.12) | collective-permute-done | bytes 393248 | tf_op jit(solution)/shard_map/ppermute | solution.py:16
  292.8 6.2 collective-permute-done.13
  300.5 6.7 collective-permute-done.14
  312.6 24.2 %all_to_all.43 = f32[2,1,128,384]{3,0,1,2:T(2,128)S(1)} all-to-all(f32[2,1,128,384]{3,0,1,2:T(2,128)S(1)} %copy.18), channel_id=1, replica_groups=mesh['seq'=128,'hid'=2] {'seq'}, dimensions={2} | all-to-all | bytes 786432 | tf_op jit(solution)/shard_map/all_to_all | solution.py:130
  338.6 17.4 %all_to_all.44 = f32[128,1,384]{2,1,0:T(1,128)S(1)} all-to-all(f32[128,1,384]{2,1,0:T(1,128)S(1)} %copy.19), channel_id=1, replica_groups=mesh['seq'=128,'hid'=2] {'seq'}, dimensions={0} | all-to-all | bytes 393216 | tf_op jit(solution)/shard_map/all_to_all | solution.py:139
  383.0 6.8 psum.31
  389.8 9.0 %reduce-scatter.7.cloned.1.call-done = f32[128,384]{1,0:T(8,128)} async-done(((f32[128,768]{1,0:T(8,128)}), f32[128,384]{1,0:T(8,128)}) %reduce-scatter.7.cloned.1.call-update) | async-done | bytes 196624 | tf_op jit(solution)/shard_map/reduce_scatter | solution.py:201
  400.6 274.9 %all-reduce.3.cloned.1.call-done = f32[768,3072]{1,0:T(8,128)} async-done(((f32[768,3072]{1,0:T(8,128)}), f32[768,3072]{1,0:T(8,128)}) %all-reduce.3.cloned.1.call-update) | async-done | bytes 9437200
  (199 shorter events, 137.0 us)
Async XLA Ops:
  7.2 190.6 %copy-start = (bf16[768,1536]{1,0:T(8,128)(2,1)S(1)}, bf16[768,1536]{1,0:T(8,128)(2,1)}, u32[]{:S(2)}) copy-start(bf16[768,1536]{1,0:T(8,128)(2,1)} %param.17) | copy-start | bytes 7077892
  18.6 2.3 collective-permute-start
  21.1 16.6 %collective-permute-start.1 = (f32[128,384]{1,0:T(8,128)S(1)}, f32[128,384]{1,0:T(8,128)S(1)}, u32[]{:S(2)}, u32[]{:S(2)}) collective-permute-start(f32[128,384]{1,0:T(8,128)S(1)} %multiply_bitcast_fusion), channel_id=1, source_target_pairs={{0,128},{2,130},{4,132},{6,134},{8,136},{10,138},{12,140},{14,142}... | collective-permute-start | bytes 589832 | tf_op jit(solution)/shard_map/ppermute | solution.py:16
  38.5 19.6 %collective-permute-start.2 = (f32[2,128,384]{2,1,0:T(8,128)}, f32[2,128,384]{2,1,0:T(8,128)}, u32[]{:S(2)}, u32[]{:S(2)}) collective-permute-start(f32[2,128,384]{2,1,0:T(8,128)} %pad_maximum_fusion.4), channel_id=1, source_target_pairs={{0,64},{2,66},{4,68},{6,70},{8,72},{10,74},{12,76},{14,78},{16,80}... | collective-permute-start | bytes 1179656 | tf_op jit(solution)/shard_map/ppermute | solution.py:16
  61.8 8.7 %collective-permute-start.3 = (f32[2,128,384]{2,1,0:T(8,128)}, f32[2,128,384]{2,1,0:T(8,128)}, u32[]{:S(2)}, u32[]{:S(2)}) collective-permute-start(f32[2,128,384]{2,1,0:T(8,128)} %maximum_select_fusion), channel_id=1, source_target_pairs={{0,32},{2,34},{4,36},{6,38},{8,40},{10,42},{12,44},{14,46},{16,48}... | collective-permute-start | bytes 1179656 | tf_op jit(solution)/shard_map/ppermute | solution.py:16
  73.9 14.1 %collective-permute-start.4 = (f32[2,128,384]{2,1,0:T(8,128)}, f32[2,128,384]{2,1,0:T(8,128)S(1)}, u32[]{:S(2)}, u32[]{:S(2)}) collective-permute-start(f32[2,128,384]{2,1,0:T(8,128)} %maximum_select_fusion.1), channel_id=1, source_target_pairs={{0,16},{2,18},{4,20},{6,22},{8,24},{10,26},{12,28},{14,30},{16,0},... | collective-permute-start | bytes 1179656 | tf_op jit(solution)/shard_map/ppermute | solution.py:16
  90.4 8.8 %collective-permute-start.5 = (f32[2,128,384]{2,1,0:T(8,128)S(1)}, f32[2,128,384]{2,1,0:T(8,128)}, u32[]{:S(2)}, u32[]{:S(2)}) collective-permute-start(f32[2,128,384]{2,1,0:T(8,128)S(1)} %maximum_select_fusion.2), channel_id=1, source_target_pairs={{0,8},{2,10},{4,12},{6,14},{8,0},{10,2},{12,4},{14,6},{16,24},{18,... | collective-permute-start | bytes 1179656 | tf_op jit(solution)/shard_map/ppermute | solution.py:16
  101.6 9.4 %collective-permute-start.6 = (f32[2,128,384]{2,1,0:T(8,128)S(1)}, f32[2,128,384]{2,1,0:T(8,128)}, u32[]{:S(2)}, u32[]{:S(2)}) collective-permute-start(f32[2,128,384]{2,1,0:T(8,128)S(1)} %maximum_select_fusion.3), channel_id=1, source_target_pairs={{0,4},{2,6},{4,0},{6,2},{8,12},{10,14},{12,8},{14,10},{16,20},{18,... | collective-permute-start | bytes 1179656 | tf_op jit(solution)/shard_map/ppermute | solution.py:16
  113.9 6.8 collective-permute-start.7
  128.9 25.9 %all-to-all-start = ((f32[2,1,128,384]{3,0,1,2:T(2,128)}), f32[2,1,128,384]{3,0,1,2:T(2,128)}, u32[]{:S(2)}, u32[]{:S(2)}) async-start(f32[2,1,128,384]{3,0,1,2:T(2,128)} %copy.16), calls=%async_computation | async-start | bytes 786432 | tf_op jit(solution)/shard_map/all_to_all | solution.py:130
  141.2 49.3 %reduce-scatter.5.cloned.1.call-start = ((), (), s32[]{:S(2)}) async-start(), calls=%async_computation.8 | async-start | bytes 589824 | tf_op jit(solution)/shard_map/reduce_scatter | solution.py:190
  176.8 40.2 %reduce-scatter.9.cloned.1.call-start = ((), (), s32[]{:S(2)}) async-start(), calls=%async_computation.10 | async-start | bytes 589824 | tf_op jit(solution)/shard_map/reduce_scatter | solution.py:216
  202.4 179.4 %reduce-scatter.11.cloned.1.call-start = ((), (), s32[]{:S(2)}) async-start(), calls=%async_computation.11 | async-start | bytes 589824 | tf_op jit(solution)/shard_map/reduce_scatter | solution.py:245
  225.0 12.1 %collective-permute-start.8 = (f32[128,384]{1,0:T(8,128)S(1)}, f32[128,384]{1,0:T(8,128)S(1)}, u32[]{:S(2)}, u32[]{:S(2)}) collective-permute-start(f32[128,384]{1,0:T(8,128)S(1)} %get-tuple-element.50), channel_id=1, source_target_pairs={{0,128},{2,130},{4,132},{6,134},{8,136},{10,138},{12,140},{14,142}... | collective-permute-start | bytes 589832 | tf_op jit(solution)/shard_map/ppermute | solution.py:16
  237.2 22.3 %collective-permute-start.9 = (f32[2,128,384]{2,1,0:T(8,128)S(1)}, f32[2,128,384]{2,1,0:T(8,128)S(1)}, u32[]{:S(2)}, u32[]{:S(2)}) collective-permute-start(f32[2,128,384]{2,1,0:T(8,128)S(1)} %pad_maximum_fusion.5), channel_id=1, source_target_pairs={{0,64},{2,66},{4,68},{6,70},{8,72},{10,74},{12,76},{14,78},{16,80}... | collective-permute-start | bytes 1179656 | tf_op jit(solution)/shard_map/ppermute | solution.py:16
  259.6 10.3 %collective-permute-start.10 = (f32[2,128,384]{2,1,0:T(8,128)S(1)}, f32[2,128,384]{2,1,0:T(8,128)S(1)}, u32[]{:S(2)}, u32[]{:S(2)}) collective-permute-start(f32[2,128,384]{2,1,0:T(8,128)S(1)} %maximum_select_fusion.6), channel_id=1, source_target_pairs={{0,32},{2,34},{4,36},{6,38},{8,40},{10,42},{12,44},{14,46},{16,48}... | collective-permute-start | bytes 1179656 | tf_op jit(solution)/shard_map/ppermute | solution.py:16
  270.1 10.9 %collective-permute-start.11 = (f32[2,128,384]{2,1,0:T(8,128)S(1)}, f32[2,128,384]{2,1,0:T(8,128)S(1)}, u32[]{:S(2)}, u32[]{:S(2)}) collective-permute-start(f32[2,128,384]{2,1,0:T(8,128)S(1)} %maximum_select_fusion.7), channel_id=1, source_target_pairs={{0,16},{2,18},{4,20},{6,22},{8,24},{10,26},{12,28},{14,30},{16,0},... | collective-permute-start | bytes 1179656 | tf_op jit(solution)/shard_map/ppermute | solution.py:16
  281.2 8.5 %collective-permute-start.12 = (f32[2,128,384]{2,1,0:T(8,128)S(1)}, f32[2,128,384]{2,1,0:T(8,128)S(1)}, u32[]{:S(2)}, u32[]{:S(2)}) collective-permute-start(f32[2,128,384]{2,1,0:T(8,128)S(1)} %maximum_select_fusion.8), channel_id=1, source_target_pairs={{0,8},{2,10},{4,12},{6,14},{8,0},{10,2},{12,4},{14,6},{16,24},{18,... | collective-permute-start | bytes 1179656 | tf_op jit(solution)/shard_map/ppermute | solution.py:16
  289.8 9.2 %collective-permute-start.13 = (f32[2,128,384]{2,1,0:T(8,128)S(1)}, f32[2,128,384]{2,1,0:T(8,128)S(1)}, u32[]{:S(2)}, u32[]{:S(2)}) collective-permute-start(f32[2,128,384]{2,1,0:T(8,128)S(1)} %maximum_select_fusion.9), channel_id=1, source_target_pairs={{0,4},{2,6},{4,0},{6,2},{8,12},{10,14},{12,8},{14,10},{16,20},{18,... | collective-permute-start | bytes 1179656 | tf_op jit(solution)/shard_map/ppermute | solution.py:16
  299.2 8.0 %collective-permute-start.14 = (f32[2,128,384]{2,1,0:T(8,128)S(1)}, f32[2,128,384]{2,1,0:T(8,128)S(1)}, u32[]{:S(2)}, u32[]{:S(2)}) collective-permute-start(f32[2,128,384]{2,1,0:T(8,128)S(1)} %maximum_select_fusion.10), channel_id=1, source_target_pairs={{0,2},{2,0},{4,6},{6,4},{8,10},{10,8},{12,14},{14,12},{16,18},{18,... | collective-permute-start | bytes 1179656 | tf_op jit(solution)/shard_map/ppermute | solution.py:16
  356.0 4.7 collective-permute-start.15
  362.4 36.4 %reduce-scatter.7.cloned.1.call-start = ((), (), s32[]{:S(2)}) async-start(), calls=%async_computation.9 | async-start | bytes 589824 | tf_op jit(solution)/shard_map/reduce_scatter | solution.py:201
  368.9 306.6 %all-reduce.3.cloned.1.call-start = ((), (), s32[]{:S(2)}) async-start(), calls=%async_computation.12 | async-start | bytes 18874368
  376.1 301.1 %copy-start.1 = (bf16[768,1536]{1,0:T(8,128)(2,1)S(1)}, bf16[768,1536]{1,0:T(8,128)(2,1)}, u32[]{:S(2)}) copy-start(bf16[768,1536]{1,0:T(8,128)(2,1)} %param.17) | copy-start | bytes 7077892
  (27 other events, 331.2 us)
Sparse Core Ops, SparseCore 0:
  176.9 13.4 reduce-scatter.4
  202.6 14.3 reduce-scatter.8
  362.5 19.3 reduce-scatter.10
  384.4 14.3 reduce-scatter.6
  404.2 271.2 all-reduce.2
where the time goes:
time: 693 us; the launch traced here: 684 us
  waiting for transfers between devices  446 us (64%)
  blocking collectives  91.2 us (13%)
  starting transfers between devices  57.5 us (8%)
  other arithmetic  34.8 us (5%)
  matrix products  29 us (4%)
  between operations  16.4 us (2%)
  local copies, waits for them, and re-layouts  8.49 us (1%)
    unnamed x6, waiting for transfers between devices  275 us
    ppermute x14, waiting for transfers between devices, partner_2(): return lax.ppermute(value, axis, pairs)  122 us
    ppermute x14, starting transfers between devices, partner_2(): return lax.ppermute(value, axis, pairs)  42.2 us
    all_to_all x2, blocking collectives, inverse_transform(): lax.all_to_all(real_out, 'seq', split_axis=0, concat_axis=0, tiled=True)  34.8 us
    all_to_all x1, blocking collectives, inverse_transform(): lax.all_to_all(twisted.reshape(2, 1, row_count, chan_count), 'seq', split...  24.2 us
    reduce_scatter x1, waiting for transfers between devices, local(): lax.psum_scatter(back_terms, 'hid', scatter_dimension=1, tiled=True)  14.5 us
  transfers between devices with their start and end apart: 22, of which 22 were waited for; matrix products, arithmetic and copies ran while one was open for 2% of the time, Pallas kernels for 0%

commit v1 on v0

v1 whole, which is shorter than its diff:
```python
import math

import jax
import jax.numpy as jnp
import ml_dtypes
import numpy as np
from jax import lax
from jax.experimental import pallas as pl
from jax.experimental.pallas import tpu as pltpu
from jax.sharding import PartitionSpec as P

EPSILON = 1e-05
GELU_SCALE = 0.7978845608028654
MESH = pl.DeviceIdType.MESH
F32 = jnp.float32
BF16 = jnp.bfloat16
GRIDS = {128: (8, 4, 4), 8: (2, 2, 2), 16: (2, 4, 2)}
TOK = 128
HALO = 16


def up_to(value, unit):
    return -(-value // unit) * unit


class Names:
    def __getattr__(self, key):
        return key


class Box(dict):
    __getattr__ = dict.__getitem__


S = Names()


class Plan:
    def __init__(self, count, width, units):
        self.n = count
        self.Z, self.X, self.Y = GRIDS[count]
        self.P = self.X * self.Y
        self.D = width
        self.C = width // 2
        self.F = units
        self.KC = self.C // count
        self.KP = self.KC
        while (self.Z * self.KP) % 16:
            self.KP += 1
        self.R = count * self.KP
        self.ZB = self.C // self.Z
        self.PB = self.Z * self.KP
        self.E = width // count
        self.EP = up_to(self.E, 8)
        self.Q3 = up_to(2 * self.Z * self.E, 128)


def tables(plan):
    n, Z, X, Y, PP = plan.n, plan.Z, plan.X, plan.Y, plan.P
    KC, KP, R = plan.KC, plan.KP, plan.R
    bits = n.bit_length() - 1
    rev = np.array([int(format(q, f"0{bits}b")[::-1], 2) for q in range(n)])
    rows = np.arange(R)
    slot = rows % KP
    source = (rows // KP) % Z * PP + rows // (KP * Z)
    freq = rev[source]
    same = (slot[:, None] == slot[None, :]) & (slot[:, None] < KC)
    angle = 2 * np.pi * ((freq[:, None] * source[None, :]) % n) / n
    first = np.concatenate([same * np.cos(angle), -(same * np.sin(angle))], axis=0)
    u = np.arange(TOK)
    twist = 2 * np.pi * ((freq[:, None] * u[None, :]) % (n * TOK)) / (n * TOK)
    table = 2 * np.pi * ((u[:, None] * u[None, :]) % TOK) / TOK
    inner = np.block([[np.cos(table), -np.sin(table)], [np.sin(table), np.cos(table)]])
    spread = np.zeros((R, plan.C))
    for p in range(PP):
        for z in range(Z):
            for i in range(KC):
                spread[(p * Z + z) * KP + i, z * plan.ZB + p * KC + i] = 1
    feat = np.arange(plan.D)
    e = feat % plan.E
    dest = feat // plan.E
    dz, dx, dy = dest // PP, dest % PP // Y, dest % Y
    up_rows = ((dx * Y + dy) * Z + dz) * plan.E + e
    down_rows = ((dy * X + dx) * Z + dz) * plan.E + e
    up_perm = np.zeros((plan.D, plan.D))
    up_perm[up_rows, feat] = 1
    down_perm = np.zeros((plan.D, plan.D))
    down_perm[down_rows, feat] = 1
    pick = np.zeros((Z * 2 * plan.EP, plan.Q3))
    for z in range(Z):
        for half in range(2):
            for k in range(plan.E):
                pick[(z * 2 + half) * plan.EP + k, half * Z * plan.E + z * plan.E + k] = 1
    half_type = ml_dtypes.bfloat16
    return dict(
        first=first.astype(half_type),
        last=first.T.astype(half_type),
        cos=np.cos(twist).astype(np.float32),
        sin=np.sin(twist).astype(np.float32),
        inner=inner.astype(half_type),
        back=inner.T.astype(half_type),
        spread=spread.astype(half_type),
        gather=spread.T.astype(half_type),
        up_perm=up_perm.astype(half_type),
        down_perm=down_perm.astype(half_type),
        pick=pick.astype(half_type),
    )


def dot(left, right):
    return jnp.dot(left, right, preferred_element_type=F32)


def dot_t(left, right):
    return lax.dot_general(left, right, (((1,), (1,)), ((), ())), preferred_element_type=F32)


TABLE_NAMES = (S.spread, S.down_perm, S.first, S.cos, S.sin, S.inner, S.back, S.last, S.gather)
TABLE_NAMES = TABLE_NAMES + (S.up_perm, S.pick)
LOAD_NAMES = (S.spec, S.ngain, S.mgain, S.tok, S.filt, S.inw, S.cot, S.outw, S.upw, S.dnw)
SEM_NAMES = (S.tok, S.halo_a, S.halo_b, S.cot, S.gain, S.outw, S.spec1, S.spec2, S.f1a, S.f2a, S.r1a, S.r2a)
SEM_NAMES = SEM_NAMES + (S.f1b, S.f2b, S.r1b, S.r2b, S.mix, S.back, S.down, S.edge, S.inp)
SEM_NAMES = SEM_NAMES + (S.inq, S.mu, S.md, S.t3 + "a", S.t3 + "b")
for step in "1234":
    for half in "ab":
        SEM_NAMES = SEM_NAMES + tuple(name + half + step for name in (S.gu, S.gd, S.u2, S.d2))
SEMS = {name: 2 * place for place, name in enumerate(SEM_NAMES)}


def make_kernel(plan):
    n, Z, X, Y, PP, D, C, F = plan.n, plan.Z, plan.X, plan.Y, plan.P, plan.D, plan.C, plan.F
    KP, R, ZB, PB, E, EP = plan.KP, plan.R, plan.ZB, plan.PB, plan.E, plan.EP
    QX, QY = D // X, D // Y
    ROW = Z * E
    inv_d = 1.0 / D

    scratch = dict(
        spec=((2, TOK, C), F32),
        ngain=((C,), F32),
        mgain=((C,), F32),
        filt=((3, 3, C), F32),
        tokf=((HALO + TOK, D), BF16),
        inb=((HALO + TOK, D), BF16),
        cotf=((TOK, D), BF16),
        gain_src=((16, C), F32),
        gains=((16, D), F32),
        inw=((3, D, C), BF16),
        outw=((D, D), BF16),
        upw=((D, F), BF16),
        dnw=((D, F), BF16),
        s0=((Z * 2 * ZB, TOK), BF16),
        r0=((Z * 2 * ZB, TOK), BF16),
        s0b=((PP * 2 * PB, TOK), BF16),
        r0b=((PP * 2 * PB, TOK), BF16),
        spec_re=((R, TOK), F32),
        spec_im=((R, TOK), F32),
        s1=((2, C, TOK), BF16),
        r1=((2, C, TOK), BF16),
        s2=((2, R, TOK), BF16),
        r2=((2, R, TOK), BF16),
        s3=((2, R, TOK), BF16),
        r3=((2, R, TOK), BF16),
        s4=((2, C, TOK), BF16),
        r4=((2, C, TOK), BF16),
        v=((2 * R, TOK), BF16),
        wave=((2 * R, TOK), F32),
        pair=((R, 2 * TOK), BF16),
        freq=((R, 2 * TOK), F32),
        shorted=((3, TOK, C), F32),
        conv=((TOK, C), F32),
        mixf=((TOK, D), BF16),
        resid=((TOK, D), F32),
        n2=((TOK, D), F32),
        mlp=((TOK, D), BF16),
        dhid=((TOK, F), F32),
        back=((TOK, D), F32),
        back_r=((TOK, D), F32),
        down=((TOK, D), F32),
        down_r=((TOK, C), F32),
        dres=((TOK, D), F32),
        dshort=((3, TOK + 8, C), F32),
        edge=((3, 8, C), F32),
        inp=((TOK, D), F32),
        inp_r=((TOK, D), F32),
        gtok=((TOK, D), F32),
        mup=((D, TOK), BF16),
        cdn=((D, TOK), BF16),
        mu=((QX, X * TOK), BF16),
        md=((QY, Y * TOK), BF16),
        gu=((X * TOK, F), BF16),
        gd=((Y * TOK, F), BF16),
        u2s=((QX, F), BF16),
        u2p=((2, 2, ROW, F // 4), BF16),
        u2r=((2, ROW, F), BF16),
        d2s=((QY, F), BF16),
        d2p=((2, 2, ROW, F // 4), BF16),
        d2r=((2, ROW, F), BF16),
        t3i=((plan.Q3, F), BF16),
        t3s=((Z * 2 * EP, F), BF16),
        t3r=((Z, 2 * EP, F), BF16),
    )
    names = list(scratch)
    shapes = tables(plan)

    def kernel(*refs):
        it = iter(refs)
        tok, ngain_h, inw_h, filt_h, spec_h, outw_h, mgain_h, upw_h, dnw_h, cot = (
            next(it) for _ in range(10)
        )
        tab_h = Box((name, next(it)) for name in TABLE_NAMES)
        out_ref, gtok_ref, gup_ref, gdn_ref = (next(it) for _ in range(4))
        b = Box((name, next(it)) for name in names)
        tab = Box((name, next(it)) for name in TABLE_NAMES)
        sems = next(it)
        loads = next(it)

        s = lax.axis_index("seq")
        h = lax.axis_index("hid")
        z = s // PP
        p = s % PP
        x = p // Y
        y = p % Y
        other = (s, 1 - h)
        nxt = lax.rem(s + 1, n)
        prv = lax.rem(s + n - 1, n)

        barrier = pltpu.get_barrier_semaphore()

        def greet(dev):
            pl.semaphore_signal(barrier, inc=1, device_id=dev, device_id_type=MESH)

        for k in sorted(range(1, Z), key=lambda k: -min(k, Z - k)):
            greet((lax.rem(z + k, Z) * PP + p, h))
        for k in range(1, PP):
            greet((z * PP + lax.rem(p + k, PP), h))
        greet(other)
        for core in range(2):
            greet((nxt, core))
            greet((prv, core))

        landing, leaving = {}, {}

        def send(src, dst, name, dev, arrives=None, leaves=None):
            k = SEMS[name]
            landing[name] = dst if arrives is None else arrives
            leaving[name] = src if leaves is None else leaves
            pltpu.make_async_remote_copy(
                src_ref=src,
                dst_ref=dst,
                send_sem=sems.at[k],
                recv_sem=sems.at[k + 1],
                device_id=dev,
                device_id_type=MESH,
            ).start()

        def got(name):
            ref = landing.pop(name)
            pltpu.make_async_copy(ref, ref, sems.at[SEMS[name] + 1]).wait()

        def sent(name):
            ref = leaving.pop(name)
            pltpu.make_async_copy(ref, ref, sems.at[SEMS[name]]).wait()

        def cols(index, size):
            return pl.ds(pl.multiple_of(index * size, 128), size)

        def rows(index, size):
            return pl.ds(pl.multiple_of(index * size, 16), size)

        own = cols(h, C)
        filt, spec = b.filt, b.spec

        load_list = [
            (spec_h, b.spec),
            (ngain_h, b.ngain),
            (mgain_h, b.mgain),
            (tok, b.tokf.at[HALO:, own]),
            (filt_h, b.filt),
            (inw_h, b.inw),
            (cot, b.cotf.at[:, own]),
            (outw_h, b.outw.at[rows(h, C)]),
            (upw_h, b.upw),
            (dnw_h, b.dnw),
        ] + [(tab_h[name], tab[name]) for name in TABLE_NAMES]
        load_at = {name: k for k, name in enumerate(LOAD_NAMES + TABLE_NAMES)}
        load_copies = [
            pltpu.make_async_copy(src, dst, loads.at[k]) for k, (src, dst) in enumerate(load_list)
        ]
        for copy in load_copies:
            copy.start()

        def loaded(*which):
            for name in which:
                load_copies[load_at[name]].wait()

        loaded(S.ngain, S.mgain)
        g16 = jnp.concatenate(
            [jnp.broadcast_to(b[name][...][None, :], (8, C)) for name in (S.ngain, S.mgain)], axis=0
        )
        b.gain_src[...] = g16
        b.gains[:, own] = g16
        loaded(S.spec)
        for part in range(2):
            turned = jnp.transpose(spec[part]).astype(BF16)
            for k in range(Z):
                at = (2 * k + part) * ZB
                b.s0[at : at + ZB, :] = turned[k * ZB : (k + 1) * ZB, :]

        pl.semaphore_wait(barrier, Z - 1 + PP - 1 + 1 + 4)

        send(tok, b.tokf.at[HALO:, own], S.tok, other)
        tail = tok.at[TOK - HALO :, :]
        send(tail, b.tokf.at[0:HALO, own], S.halo_a, (nxt, h))
        send(tail, b.tokf.at[0:HALO, own], S.halo_b, (nxt, 1 - h))
        send(b.gain_src, b.gains.at[:, own], S.gain, other)

        z_order = sorted(range(1, Z), key=lambda k: -min(k, Z - k))
        p_order = sorted(
            range(1, PP), key=lambda k: -min(k // Y, X - k // Y) - min(k % Y, Y - k % Y)
        )

        def z_send(src, dst, size, name):
            for k in z_order:
                to = lax.rem(z + k, Z)
                some = pl.ds(0, (Z - 1) * size)
                send(
                    src.at[rows(to, size)],
                    dst.at[rows(z, size)],
                    name,
                    (to * PP + p, h),
                    dst.at[some],
                    src.at[some],
                )

        def p_send(src, dst, size, name):
            for k in p_order:
                to = lax.rem(x + k // Y, X) * Y + lax.rem(y + k % Y, Y)
                some = pl.ds(0, (PP - 1) * size)
                send(
                    src.at[rows(to, size)],
                    dst.at[rows(p, size)],
                    name,
                    (z * PP + to, h),
                    dst.at[some],
                    src.at[some],
                )

        z_send(b.s0, b.r0, 2 * ZB, S.spec1)
        b.r0[rows(z, 2 * ZB), :] = b.s0[rows(z, 2 * ZB), :]
        send(cot, b.cotf.at[:, own], S.cot, other)
        send(outw_h, b.outw.at[rows(h, C)], S.outw, other)

        got(S.tok)
        got(S.halo_a)
        got(S.halo_b)
        got(S.gain)
        loaded(S.tok, S.filt, S.inw)
        norm_gain = b.gains[0:1, :]
        mlp_gain = b.gains[8:9, :]
        tokens = b.tokf[...].astype(F32)
        scale_in = lax.rsqrt(jnp.sum(tokens * tokens, axis=1, keepdims=True) * inv_d + EPSILON)
        row = lax.broadcasted_iota(jnp.int32, (HALO + TOK, 1), 0)
        keep = jnp.logical_or(row >= HALO, s > 0)
        b.inb[...] = jnp.where(keep, tokens * scale_in * norm_gain, 0.0).astype(BF16)
        for j in range(3):
            proj = dot(b.inb[...], b.inw[j])
            total = filt[j, 0:1, :] * proj
            for i in range(1, 3):
                total = total + filt[j, i : i + 1, :] * pltpu.roll(proj, i, 0)
            b.shorted[j] = total[HALO:, :]

        def conv_out(value, a, mark):
            turned = jnp.transpose(value).astype(BF16)
            b.s1[a] = turned
            b.r1[a, rows(z, ZB), :] = b.s1[a, rows(z, ZB), :]
            z_send(b.s1.at[a], b.r1.at[a], ZB, S.f1 + mark)

        def conv_plane(a, mark):
            got(S.f1 + mark)
            b.s2[a] = dot(tab.spread[...], b.r1[a]).astype(BF16)
            b.r2[a, rows(p, PB), :] = b.s2[a, rows(p, PB), :]
            p_send(b.s2.at[a], b.r2.at[a], PB, S.f2 + mark)

        def conv_work(a, mark, sign):
            got(S.f2 + mark)
            arrived = b.r2[a]
            b.wave[...] = dot(tab.first[...], arrived)
            cosine = tab.cos[...]
            sine = tab.sin[...]
            yr = b.wave[0:R, :]
            yi = b.wave[R:, :]
            b.pair[:, 0:TOK] = (yr * cosine + yi * sine).astype(BF16)
            b.pair[:, TOK:] = (yi * cosine - yr * sine).astype(BF16)
            b.freq[...] = dot(b.pair[...], tab.inner[...])
            kr = b.spec_re[...]
            ki = sign * b.spec_im[...]
            fr = b.freq[:, 0:TOK]
            fi = b.freq[:, TOK:]
            b.pair[:, 0:TOK] = (kr * fr - ki * fi).astype(BF16)
            b.pair[:, TOK:] = (kr * fi + ki * fr).astype(BF16)
            b.freq[...] = dot(b.pair[...], tab.back[...])
            wr = b.freq[:, 0:TOK]
            wi = b.freq[:, TOK:]
            b.v[0:R, :] = (wr * cosine - wi * sine).astype(BF16)
            b.v[R:, :] = (wi * cosine + wr * sine).astype(BF16)
            b.s3[a] = (dot(tab.last[...], b.v[...]) * (1.0 / (n * TOK))).astype(BF16)
            b.r3[a, rows(p, PB), :] = b.s3[a, rows(p, PB), :]
            p_send(b.s3.at[a], b.r3.at[a], PB, S.r1 + mark)

        def conv_return(a, mark):
            got(S.r1 + mark)
            b.s4[a] = dot(tab.gather[...], b.r3[a]).astype(BF16)
            b.r4[a, rows(z, ZB), :] = b.s4[a, rows(z, ZB), :]
            z_send(b.s4.at[a], b.r4.at[a], ZB, S.r2 + mark)

        def conv_in(a, mark):
            got(S.r2 + mark)
            return jnp.transpose(b.r4[a].astype(F32))

        conv_out(b.shorted[1] * b.shorted[0], 0, "a")

        loaded(S.spread)
        got(S.spec1)
        for part in range(2):
            picked = [
                b.r0[(2 * k + part) * ZB : (2 * k + part + 1) * ZB, :] for k in range(Z)
            ]
            placed = dot(tab.spread[...], jnp.concatenate(picked, axis=0)).astype(BF16)
            for k in range(PP):
                at = (2 * k + part) * PB
                b.s0b[at : at + PB, :] = placed[k * PB : (k + 1) * PB, :]
        p_send(b.s0b, b.r0b, 2 * PB, S.spec2)
        b.r0b[rows(p, 2 * PB), :] = b.s0b[rows(p, 2 * PB), :]

        conv_plane(0, "a")

        loaded(S.dnw, S.down_perm, S.cot)
        got(S.cot)
        FH = F // 2
        wide = min(FH, 256)

        @pl.loop(0, F // wide)
        def _(k):
            at = cols(k, wide)
            b.dhid[:, at] = dot(b.cotf[...], b.dnw[:, at])

        got(S.spec2)
        for k in range(PP):
            for part, name in enumerate((S.spec_re, S.spec_im)):
                at = (2 * k + part) * PB
                b[name][k * PB : (k + 1) * PB, :] = b.r0b[at : at + PB, :].astype(F32)
        loaded(S.first, S.last, S.cos, S.sin, S.inner, S.back, S.gather)
        conv_work(0, "a", 1.0)
        loaded(S.outw, S.upw, S.up_perm, S.pick)
        got(S.outw)
        b.cdn[...] = dot_t(tab.down_perm[...], b.cotf[...]).astype(BF16)
        conv_return(0, "a")
        conv = conv_in(0, "a")
        b.conv[...] = conv
        b.mixf[:, own] = (b.shorted[2] * conv).astype(BF16)
        send(b.mixf.at[:, own], b.mixf.at[:, own], S.mix, other)
        got(S.mix)

        resid = b.tokf[HALO:, :].astype(F32) + dot(b.mixf[...], b.outw[...])
        b.resid[...] = resid
        scale_two = lax.rsqrt(jnp.sum(resid * resid, axis=1, keepdims=True) * inv_d + EPSILON)
        normed = resid * scale_two
        b.n2[...] = normed
        b.mlp[...] = (normed * mlp_gain).astype(BF16)

        def at_x(k):
            return (z * PP + k * Y + y, h)

        def at_y(k):
            return (z * PP + x * Y + k, h)

        mu_all = b.mu.at[:, pl.ds(0, (X - 1) * TOK)]
        md_all = b.md.at[:, pl.ds(0, (Y - 1) * TOK)]
        HALF = TOK // 2
        FQ = FH // 2
        halves = (pl.ds(0, FH), pl.ds(FH, FH))
        marks = ("a", "b")

        def ring_start(ref, i, size, at, name, c):
            name = name + marks[c]
            if size == 2:
                block = ref.at[rows(i, TOK), halves[c]]
                send(block, block, name + "3", at(1 - i))
                return
            right, left = lax.rem(i + 1, size), lax.rem(i + size - 1, size)
            low = ref.at[rows(2 * i, HALF), halves[c]]
            high = ref.at[rows(2 * i + 1, HALF), halves[c]]
            rest = ref.at[pl.ds(0, 2 * TOK), halves[c]]
            send(low, low, name + "1", at(right))
            send(high, high, name + "2", at(left))
            send(high, high, name + "3", at(right), rest, rest)
            send(low, low, name + "3", at(left), rest, rest)

        def ring_relay(ref, i, size, at, name, c):
            name = name + marks[c]
            if size == 2:
                return
            right, left = lax.rem(i + 1, size), lax.rem(i + size - 1, size)
            rest = ref.at[pl.ds(0, 2 * TOK), halves[c]]
            got(name + "1")
            low = ref.at[rows(2 * left, HALF), halves[c]]
            send(low, low, name + "3", at(right), rest, rest)
            got(name + "2")
            high = ref.at[rows(2 * right + 1, HALF), halves[c]]
            send(high, high, name + "3", at(left), rest, rest)

        def sum_start(src, i, size, at, name, c):
            put = b[name + S.r]
            if size == 2:
                send(
                    src.at[rows(1 - i, ROW), halves[c]],
                    put.at[0, :, halves[c]],
                    name + marks[c] + "3",
                    at(1 - i),
                )
                return
            right, left = lax.rem(i + 1, size), lax.rem(i + size - 1, size)
            far_rows = rows(lax.rem(i + 2, size), ROW)
            over = b[name + S.p]
            for side, to in ((0, right), (1, left)):
                part = pl.ds(c * FH + side * FQ, FQ)
                send(
                    src.at[far_rows, part],
                    over.at[c, side],
                    name + marks[c] + "12"[side],
                    at(to),
                )

        def sum_relay(src, i, size, at, name, c):
            if size == 2:
                return
            put, over = b[name + S.r], b[name + S.p]
            right, left = lax.rem(i + 1, size), lax.rem(i + size - 1, size)
            for side, to in ((0, right), (1, left)):
                part = pl.ds(c * FH + side * FQ, FQ)
                got(name + marks[c] + "12"[side])
                more = src[rows(to, ROW), part].astype(F32) + over[c, side].astype(F32)
                src[rows(to, ROW), part] = more.astype(BF16)
                send(
                    src.at[rows(to, ROW), halves[c]],
                    put.at[side, :, halves[c]],
                    name + marks[c] + "34"[side],
                    at(to),
                )

        def sum_end(src, i, size, name, c):
            put = b[name + S.r]
            got(name + marks[c] + "3")
            total = src[rows(i, ROW), halves[c]].astype(F32) + put[0, :, halves[c]].astype(F32)
            if size == 2:
                return total
            got(name + marks[c] + "4")
            return total + put[1, :, halves[c]].astype(F32)

        def grads_relay(c):
            ring_relay(b.gu, x, X, at_x, S.gu, c)
            ring_relay(b.gd, y, Y, at_y, S.gd, c)

        def grads_local(c):
            got(S.gu + marks[c] + "3")
            if c == 0:
                got(S.mu)

            @pl.loop(c * (FH // wide), (c + 1) * (FH // wide))
            def _(k):
                at = cols(k, wide)
                b.u2s[:, at] = dot(b.mu[...], b.gu[:, at]).astype(BF16)

            sum_start(b.u2s, y, Y, at_y, S.u2, c)
            got(S.gd + marks[c] + "3")
            if c == 0:
                got(S.md)

            @pl.loop(c * (FH // wide), (c + 1) * (FH // wide))
            def _(k):
                at = cols(k, wide)
                b.d2s[:, at] = dot(b.md[...], b.gd[:, at]).astype(BF16)

            sum_start(b.d2s, x, X, at_x, S.d2, c)

        def grads_pass(c):
            sum_relay(b.u2s, y, Y, at_y, S.u2, c)
            sum_relay(b.d2s, x, X, at_x, S.d2, c)

        def grads_z(c):
            b.t3i[0:ROW, halves[c]] = sum_end(b.u2s, y, Y, S.u2, c).astype(BF16)
            b.t3i[ROW : 2 * ROW, halves[c]] = sum_end(b.d2s, x, X, S.d2, c).astype(BF16)
            if plan.Q3 > 2 * ROW:
                b.t3i[2 * ROW :, halves[c]] = jnp.zeros((plan.Q3 - 2 * ROW, FH), BF16)
            b.t3s[:, halves[c]] = dot(tab.pick[...], b.t3i[:, halves[c]]).astype(BF16)
            t3_all = b.t3r.at[pl.ds(0, Z - 1), :, halves[c]]
            for k in z_order:
                to = lax.rem(z + k, Z)
                send(
                    b.t3s.at[rows(to, 2 * EP), halves[c]],
                    b.t3r.at[z, :, halves[c]],
                    S.t3 + marks[c],
                    (to * PP + p, h),
                    t3_all,
                    t3_all,
                )
            b.t3r[z, :, halves[c]] = b.t3s[rows(z, 2 * EP), halves[c]]

        for c in range(2):

            @pl.loop(c * (FH // wide), (c + 1) * (FH // wide))
            def _(k):
                at = cols(k, wide)
                pre = dot(b.mlp[...], b.upw[:, at])
                tanh = jnp.tanh(GELU_SCALE * (pre + 0.044715 * pre * pre * pre))
                b.gd[rows(y, TOK), at] = (0.5 * pre * (1.0 + tanh)).astype(BF16)
                slope = 0.5 * (1.0 + tanh) + 0.5 * pre * (1.0 - tanh * tanh) * GELU_SCALE * (
                    1.0 + 3.0 * 0.044715 * pre * pre
                )
                b.gu[rows(x, TOK), at] = (b.dhid[:, at] * slope).astype(BF16)

            ring_start(b.gu, x, X, at_x, S.gu, c)
            ring_start(b.gd, y, Y, at_y, S.gd, c)

        hidden = b.gd.at[rows(y, TOK)]
        d_pre = b.gu.at[rows(x, TOK)]
        for k in range(D // 256):
            at = slice(k * 256, (k + 1) * 256)
            b.back[:, at] = dot_t(d_pre[...], b.upw[at, :])
        send(b.back, b.back_r, S.back, other)
        b.mup[...] = dot_t(tab.up_perm[...], b.mlp[...]).astype(BF16)
        for k in range(1, X):
            to = lax.rem(x + k, X)
            send(
                b.mup.at[rows(to, QX)],
                b.mu.at[:, cols(x, TOK)],
                S.mu,
                at_x(to),
                mu_all,
                mu_all,
            )
        for k in range(1, Y):
            to = lax.rem(y + k, Y)
            send(
                b.cdn.at[rows(to, QY)],
                b.md.at[:, cols(y, TOK)],
                S.md,
                at_y(to),
                md_all,
                md_all,
            )
        b.mu[:, cols(x, TOK)] = b.mup[rows(x, QX), :]
        b.md[:, cols(y, TOK)] = b.cdn[rows(y, QY), :]

        got(S.back)
        d_n2 = (b.back[...] + b.back_r[...]) * mlp_gain
        normed = b.n2[...]
        inner = jnp.sum(d_n2 * normed, axis=1, keepdims=True) * inv_d
        d_resid = b.cotf[...].astype(F32) + scale_two * (d_n2 - normed * inner)
        b.dres[...] = d_resid
        d_mixed = dot_t(d_resid.astype(BF16), b.outw[rows(h, C), :])
        d_outer = d_mixed * b.conv[...]
        b.dshort[2, 0:TOK, :] = d_outer
        conv_out(d_mixed * b.shorted[2], 1, "b")

        grads_relay(0)
        conv_plane(1, "b")
        grads_relay(1)

        for k in range(D // 256):
            at = slice(k * 256, (k + 1) * 256)
            b.down[:, at] = dot_t(hidden[...], b.dnw[at, :])
        send(b.down.at[:, cols(1 - h, C)], b.down_r, S.down, other)
        got(S.down)
        out_ref[...] = (b.resid[:, own] + b.down[:, own] + b.down_r[...]).astype(BF16)
        conv_work(1, "b", -1.0)

        grads_local(0)
        conv_return(1, "b")
        grads_local(1)
        grads_pass(0)
        d_signal = conv_in(1, "b")
        b.dshort[0, 0:TOK, :] = d_signal * b.shorted[1]
        b.dshort[1, 0:TOK, :] = d_signal * b.shorted[0]
        for j in range(3):
            b.edge[j] = b.dshort[j, 0:8, :]
        send(b.edge, b.dshort.at[:, TOK:, :], S.edge, (prv, h))
        grads_z(0)
        grads_pass(1)

        MAIN = TOK - HALO
        for j in range(3):
            value = b.dshort[j, 0:TOK, :]
            total = filt[j, 0:1, :] * value
            for i in range(1, 3):
                total = total + filt[j, i : i + 1, :] * pltpu.roll(value, TOK - i, 0)
            part = dot_t(total[0:MAIN, :].astype(BF16), b.inw[j])
            if j == 0:
                b.inp[0:MAIN, :] = part
            else:
                b.inp[0:MAIN, :] += part
        send(b.inp.at[0:MAIN], b.inp_r.at[0:MAIN], S.inp, other)
        got(S.edge)
        last = s == n - 1
        row = lax.broadcasted_iota(jnp.int32, (HALO + 8, 1), 0)
        keep = jnp.logical_or(row < HALO, jnp.logical_not(last))
        for j in range(3):
            value = jnp.where(keep, b.dshort[j, MAIN:, :], 0.0)
            total = filt[j, 0:1, :] * value
            for i in range(1, 3):
                total = total + filt[j, i : i + 1, :] * pltpu.roll(value, HALO + 8 - i, 0)
            part = dot_t(total[0:HALO, :].astype(BF16), b.inw[j])
            if j == 0:
                b.inp[MAIN:, :] = part
            else:
                b.inp[MAIN:, :] += part
        send(b.inp.at[MAIN:], b.inp_r.at[MAIN:], S.inq, other)
        grads_z(1)
        got(S.inq)
        got(S.inp)
        d_n1 = (b.inp[...] + b.inp_r[...]) * norm_gain
        tokens = b.tokf[HALO:, :].astype(F32)
        scale_in = lax.rsqrt(jnp.sum(tokens * tokens, axis=1, keepdims=True) * inv_d + EPSILON)
        normed = tokens * scale_in
        inner = jnp.sum(d_n1 * normed, axis=1, keepdims=True) * inv_d
        b.gtok[...] = b.dres[...] + scale_in * (d_n1 - normed * inner)
        gtok_ref[...] = b.gtok[:, own].astype(BF16)

        got(S.t3 + "a")
        got(S.t3 + "b")
        total = b.t3r[0].astype(F32)
        for k in range(1, Z):
            total = total + b.t3r[k].astype(F32)
        total = total * (1.0 / math.sqrt(n * TOK))
        gup_ref[...] = total[0:E, :]
        gdn_ref[...] = total[EP : EP + E, :]

        for name in list(leaving):
            sent(name)

    table_scratch = [pltpu.VMEM(shapes[name].shape, shapes[name].dtype) for name in TABLE_NAMES]
    scratch_shapes = (
        [pltpu.VMEM(*scratch[name]) for name in names]
        + table_scratch
        + [
            pltpu.SemaphoreType.DMA((2 * len(SEM_NAMES),)),
            pltpu.SemaphoreType.DMA((len(LOAD_NAMES) + len(TABLE_NAMES),)),
        ]
    )
    return kernel, scratch_shapes, shapes


def solution(mesh):
    count = mesh.shape["seq"]

    def local(tokens, norm_gain, in_weight, filters, spectrum, out_weight, mlp_gain, up, down, cot):
        rows, chans = tokens.shape
        plan = Plan(count, 2 * chans, up.shape[1])
        kernel, scratch_shapes, constants = make_kernel(plan)
        here = pl.BlockSpec(memory_space=pltpu.VMEM)
        far = pl.BlockSpec(memory_space=pl.ANY)
        in_specs = [far] * (10 + len(TABLE_NAMES))
        made = pl.pallas_call(
            kernel,
            out_shape=(
                jax.ShapeDtypeStruct((rows, chans), BF16),
                jax.ShapeDtypeStruct((rows, chans), BF16),
                jax.ShapeDtypeStruct((plan.E, plan.F), F32),
                jax.ShapeDtypeStruct((plan.E, plan.F), F32),
            ),
            in_specs=in_specs,
            out_specs=(here, here, here, here),
            scratch_shapes=scratch_shapes,
            compiler_params=pltpu.CompilerParams(
                collective_id=0, has_side_effects=True, vmem_limit_bytes=58 * 1024 * 1024
            ),
        )(
            tokens,
            norm_gain,
            in_weight,
            filters,
            spectrum,
            out_weight,
            mlp_gain,
            up,
            down,
            cot,
            *[constants[name] for name in TABLE_NAMES],
        )

        def hand_over(*refs):
            for k in range(4):
                refs[k + 4][...] = refs[k][...]

        return pl.pallas_call(
            hand_over,
            out_shape=tuple(jax.ShapeDtypeStruct(part.shape, part.dtype) for part in made),
            in_specs=[here] * 4,
            out_specs=(here,) * 4,
        )(*made)

    return jax.shard_map(
        local,
        mesh=mesh,
        in_specs=(
            P("seq", "hid"),
            P("hid"),
            P(None, None, "hid"),
            P(None, None, "hid"),
            P(None, "seq", "hid"),
            P("hid", None),
            P("hid"),
            P(None, "hid"),
            P(None, "hid"),
            P("seq", "hid"),
        ),
        out_specs=(P("seq", "hid"), P("seq", "hid"), P("seq", "hid"), P("seq", "hid")),
        check_vma=False,
    )
```

time: 693 us -> 85.5 us (0.12); the launches traced: 684 us -> 85.3 us
  waiting for transfers between devices: 446 us -> 0 us
  blocking collectives: 91.2 us -> 0 us
  Pallas kernels: 0 us -> 84.7 us
  starting transfers between devices: 57.5 us -> 0 us
  other arithmetic: 34.8 us -> 0 us
  matrix products: 29 us -> 0 us
  between operations: 16.4 us -> 0.64 us
  local copies, waits for them, and re-layouts: 8.49 us -> 0 us
    unnamed x6 -> x0, waiting for transfers between devices: 275 us -> none
    ppermute x16 -> x0, waiting for transfers between devices: 126 us -> none  [the longest x14 122 us: partner_2(): return lax.ppermute(value, axis, pairs)]
    pallas_call x0 -> x2, Pallas kernels: none -> 84.7 us  [the longest x1 83 us: local(): pl.pallas_call(kernel, out_shape=(jax.ShapeDtypeStruct((rows, chans), BF1...]
    all_to_all x3 -> x0, blocking collectives: 59 us -> none  [the longest x2 34.8 us: inverse_transform(): lax.all_to_all(real_out, 'seq', split_axis=0, concat_axis=0, tiled=True)]
    ppermute x16 -> x0, starting transfers between devices: 44.9 us -> none  [the longest x14 42.2 us: partner_2(): return lax.ppermute(value, axis, pairs)]
    reduce_scatter x4 -> x0, waiting for transfers between devices: 31.7 us -> none  [the longest x1 14.5 us: local(): lax.psum_scatter(back_terms, 'hid', scatter_dimension=1, tiled=True)]
    dot_general x30 -> x0, matrix products: 29 us -> none  [the longest x20 11.9 us: precise_dot(): jnp.dot(left, right, precision=PRECISE, preferred_element_type=jnp.float32)]
    psum x4 -> x0, blocking collectives: 17.1 us -> none  [the longest x1 6.79 us: local(): inner_one = lax.psum(jnp.sum(d_n1 * normed_in, axis=1), 'hid') / model_width]
  transfers between devices with their start and end apart: 22 -> 0, of which waited for: 22 -> 0; matrix products, arithmetic and copies ran while one was open for 2% -> 0% of each run, Pallas kernels for 0% -> 0%
where the time goes in v1:
time: 85.5 us; the launch traced here: 85.3 us
  Pallas kernels  84.7 us (99%)
    pallas_call x1, Pallas kernels, local(): pl.pallas_call(kernel, out_shape=(jax.ShapeDtypeStruct((rows, chans), BF1...  83 us

profile of v1, /device:TPU:1, one launch (start us, length us, event | category | flops | bytes accessed | tf_op | source)
XLA Modules:
  0.0 85.3 jit_solution(12053636246617712516)
XLA Ops:
  0.6 83.0 %shard_map.228 = (bf16[128,384]{1,0:T(8,128)(2,1)}, bf16[128,384]{1,0:T(8,128)(2,1)}, f32[6,1536]{1,0:T(8,128)}, f32[6,1536]{1,0:T(8,128)}) custom-call(bf16[128,384]{1,0:T(8,128)(2,1)} %refs_0_.1, f32[384]{0:T(512)} %refs_1_.1, bf16[3,768,384]{2,1,0:T(8,128)(2,1)} %refs_2_.1, f32[3,3,384]{2,1,0:T(4,128)} %refs_3_.1, f32[2,128,384]{2,1,0:T(8,128)} %refs_4_.1, ...), custom_call_target="tpu_custom_call" | custom-call | tf_op jit(solution)/shard_map/pallas_call | solution.py:763
  83.7 1.7 %shard_map.229 = (bf16[128,384]{1,0:T(8,128)(2,1)}, bf16[128,384]{1,0:T(8,128)(2,1)}, f32[6,1536]{1,0:T(8,128)}, f32[6,1536]{1,0:T(8,128)}) custom-call(bf16[128,384]{1,0:T(8,128)(2,1)} %get-tuple-element.8.refs_0_, bf16[128,384]{1,0:T(8,128)(2,1)} %get-tuple-element.9.refs_1_, f32[6,1536]{1,0:T(8,128)} %get-tuple-element.10.refs_2_, ...), custom_call_target="tpu_custom_call" | custom-call | tf_op jit(solution)/shard_map/pallas_call | solution.py:795

commit v2 on v1

--- a/solution.py
+++ b/solution.py
@@ -17,10 +17,6 @@
 GRIDS = {128: (8, 4, 4), 8: (2, 2, 2), 16: (2, 4, 2)}
 TOK = 128
 HALO = 16
-
-
-def up_to(value, unit):
-    return -(-value // unit) * unit
 
 
 class Names:
@@ -51,8 +47,8 @@
         self.ZB = self.C // self.Z
         self.PB = self.Z * self.KP
         self.E = width // count
-        self.EP = up_to(self.E, 8)
-        self.Q3 = up_to(2 * self.Z * self.E, 128)
+        self.G = 4
+        self.TR = self.G * 2 * self.E
 
 
 def tables(plan):
@@ -86,11 +82,13 @@
     up_perm[up_rows, feat] = 1
     down_perm = np.zeros((plan.D, plan.D))
     down_perm[down_rows, feat] = 1
-    pick = np.zeros((Z * 2 * plan.EP, plan.Q3))
-    for z in range(Z):
+    pick = np.zeros((Z * plan.TR, Z * plan.TR))
+    for g in range(plan.G):
         for half in range(2):
-            for k in range(plan.E):
-                pick[(z * 2 + half) * plan.EP + k, half * Z * plan.E + z * plan.E + k] = 1
+            for z in range(Z):
+                for k in range(plan.E):
+                    to = ((z * plan.G + g) * 2 + half) * plan.E + k
+                    pick[to, ((g * 2 + half) * Z + z) * plan.E + k] = 1
     half_type = ml_dtypes.bfloat16
     return dict(
         first=first.astype(half_type),
@@ -129,7 +127,7 @@
 
 def make_kernel(plan):
     n, Z, X, Y, PP, D, C, F = plan.n, plan.Z, plan.X, plan.Y, plan.P, plan.D, plan.C, plan.F
-    KP, R, ZB, PB, E, EP = plan.KP, plan.R, plan.ZB, plan.PB, plan.E, plan.EP
+    KP, R, ZB, PB, E, G, TR = plan.KP, plan.R, plan.ZB, plan.PB, plan.E, plan.G, plan.TR
     QX, QY = D // X, D // Y
     ROW = Z * E
     inv_d = 1.0 / D
@@ -190,14 +188,14 @@
         gu=((X * TOK, F), BF16),
         gd=((Y * TOK, F), BF16),
         u2s=((QX, F), BF16),
-        u2p=((2, 2, ROW, F // 4), BF16),
+        u2p=((2, ROW, F // 2), BF16),
         u2r=((2, ROW, F), BF16),
         d2s=((QY, F), BF16),
-        d2p=((2, 2, ROW, F // 4), BF16),
+        d2p=((2, ROW, F // 2), BF16),
         d2r=((2, ROW, F), BF16),
-        t3i=((plan.Q3, F), BF16),
-        t3s=((Z * 2 * EP, F), BF16),
-        t3r=((Z, 2 * EP, F), BF16),
+        t3i=((Z * TR, F // G), BF16),
+        t3s=((Z * TR, F // G), BF16),
+        t3r=((Z, TR, F // G), BF16),
     )
     names = list(scratch)
     shapes = tables(plan)
@@ -436,8 +434,9 @@
 
         loaded(S.dnw, S.down_perm, S.cot)
         got(S.cot)
-        FH = F // 2
-        wide = min(FH, 256)
+        FB = F // 3 if F % 384 == 0 else F // 2
+        begins, sizes = (0, F - FB), (F - FB, FB)
+        wide = min(FB, 256)
 
         @pl.loop(0, F // wide)
         def _(k):
@@ -453,7 +452,26 @@
         conv_work(0, "a", 1.0)
         loaded(S.outw, S.upw, S.up_perm, S.pick)
         got(S.outw)
+        def at_x(k):
+            return (z * PP + k * Y + y, h)
+
+        def at_y(k):
+            return (z * PP + x * Y + k, h)
+
+        mu_all = b.mu.at[:, pl.ds(0, (X - 1) * TOK)]
+        md_all = b.md.at[:, pl.ds(0, (Y - 1) * TOK)]
         b.cdn[...] = dot_t(tab.down_perm[...], b.cotf[...]).astype(BF16)
+        for k in range(1, Y):
+            to = lax.rem(y + k, Y)
+            send(
+                b.cdn.at[rows(to, QY)],
+                b.md.at[:, cols(y, TOK)],
+                S.md,
+                at_y(to),
+                md_all,
+                md_all,
+            )
+        b.md[:, cols(y, TOK)] = b.cdn[rows(y, QY), :]
         conv_return(0, "a")
         conv = conv_in(0, "a")
         b.conv[...] = conv
@@ -468,17 +486,9 @@
         b.n2[...] = normed
         b.mlp[...] = (normed * mlp_gain).astype(BF16)
 
-        def at_x(k):
-            return (z * PP + k * Y + y, h)
-
-        def at_y(k):
-            return (z * PP + x * Y + k, h)
-
-        mu_all = b.mu.at[:, pl.ds(0, (X - 1) * TOK)]
-        md_all = b.md.at[:, pl.ds(0, (Y - 1) * TOK)]
         HALF = TOK // 2
-        FQ = FH // 2
-        halves = (pl.ds(0, FH), pl.ds(FH, FH))
+        halves = tuple(pl.ds(begin, size) for begin, size in zip(begins, sizes))
+        thin = tuple(pl.ds(begin // G, size // G) for begin, size in zip(begins, sizes))
         marks = ("a", "b")
 
         def ring_start(ref, i, size, at, name, c):
@@ -490,9 +500,17 @@
             right, left = lax.rem(i + 1, size), lax.rem(i + size - 1, size)
             low = ref.at[rows(2 * i, HALF), halves[c]]
             high = ref.at[rows(2 * i + 1, HALF), halves[c]]
-            rest = ref.at[pl.ds(0, 2 * TOK), halves[c]]
             send(low, low, name + "1", at(right))
             send(high, high, name + "2", at(left))
+
+        def ring_rest(ref, i, size, at, name, c):
+            name = name + marks[c]
+            if size == 2:
+                return
+            right, left = lax.rem(i + 1, size), lax.rem(i + size - 1, size)
+            low = ref.at[rows(2 * i, HALF), halves[c]]
+            high = ref.at[rows(2 * i + 1, HALF), halves[c]]
+            rest = ref.at[pl.ds(0, 2 * TOK), halves[c]]
             send(high, high, name + "3", at(right), rest, rest)
             send(low, low, name + "3", at(left), rest, rest)
 
@@ -523,10 +541,10 @@
             far_rows = rows(lax.rem(i + 2, size), ROW)
             over = b[name + S.p]
             for side, to in ((0, right), (1, left)):
-                part = pl.ds(c * FH + side * FQ, FQ)
+                part = pl.ds(begins[c] + side * (sizes[c] // 2), sizes[c] // 2)
                 send(
                     src.at[far_rows, part],
-                    over.at[c, side],
+                    over.at[side, :, pl.ds(begins[c] // 2, sizes[c] // 2)],
                     name + marks[c] + "12"[side],
                     at(to),
                 )
@@ -537,9 +555,10 @@
             put, over = b[name + S.r], b[name + S.p]
             right, left = lax.rem(i + 1, size), lax.rem(i + size - 1, size)
             for side, to in ((0, right), (1, left)):
-                part = pl.ds(c * FH + side * FQ, FQ)
+                part = pl.ds(begins[c] + side * (sizes[c] // 2), sizes[c] // 2)
                 got(name + marks[c] + "12"[side])
-                more = src[rows(to, ROW), part].astype(F32) + over[c, side].astype(F32)
+                came = over[side, :, pl.ds(begins[c] // 2, sizes[c] // 2)]
+                more = src[rows(to, ROW), part].astype(F32) + came.astype(F32)
                 src[rows(to, ROW), part] = more.astype(BF16)
                 send(
                     src.at[rows(to, ROW), halves[c]],
@@ -566,7 +585,7 @@
             if c == 0:
                 got(S.mu)
 
-            @pl.loop(c * (FH // wide), (c + 1) * (FH // wide))
+            @pl.loop(begins[c] // wide, (begins[c] + sizes[c]) // wide)
             def _(k):
                 at = cols(k, wide)
                 b.u2s[:, at] = dot(b.mu[...], b.gu[:, at]).astype(BF16)
@@ -576,7 +595,7 @@
             if c == 0:
                 got(S.md)
 
-            @pl.loop(c * (FH // wide), (c + 1) * (FH // wide))
+            @pl.loop(begins[c] // wide, (begins[c] + sizes[c]) // wide)
             def _(k):
                 at = cols(k, wide)
                 b.d2s[:, at] = dot(b.md[...], b.gd[:, at]).astype(BF16)
@@ -588,27 +607,42 @@
             sum_relay(b.d2s, x, X, at_x, S.d2, c)
 
         def grads_z(c):
-            b.t3i[0:ROW, halves[c]] = sum_end(b.u2s, y, Y, S.u2, c).astype(BF16)
-            b.t3i[ROW : 2 * ROW, halves[c]] = sum_end(b.d2s, x, X, S.d2, c).astype(BF16)
-            if plan.Q3 > 2 * ROW:
-                b.t3i[2 * ROW :, halves[c]] = jnp.zeros((plan.Q3 - 2 * ROW, FH), BF16)
-            b.t3s[:, halves[c]] = dot(tab.pick[...], b.t3i[:, halves[c]]).astype(BF16)
-            t3_all = b.t3r.at[pl.ds(0, Z - 1), :, halves[c]]
+            width = sizes[c] // G
+            for half, total in enumerate(
+                (sum_end(b.u2s, y, Y, S.u2, c), sum_end(b.d2s, x, X, S.d2, c))
+            ):
+                for g in range(G):
+                    at = (g * 2 + half) * ROW
+                    b.t3i[at : at + ROW, thin[c]] = total[:, g * width : (g + 1) * width].astype(BF16)
+            b.t3s[:, thin[c]] = dot(tab.pick[...], b.t3i[:, thin[c]]).astype(BF16)
+            t3_all = b.t3r.at[pl.ds(0, Z - 1), :, thin[c]]
             for k in z_order:
                 to = lax.rem(z + k, Z)
                 send(
-                    b.t3s.at[rows(to, 2 * EP), halves[c]],
-                    b.t3r.at[z, :, halves[c]],
+                    b.t3s.at[rows(to, TR), thin[c]],
+                    b.t3r.at[z, :, thin[c]],
                     S.t3 + marks[c],
                     (to * PP + p, h),
                     t3_all,
                     t3_all,
                 )
-            b.t3r[z, :, halves[c]] = b.t3s[rows(z, 2 * EP), halves[c]]
+            b.t3r[z, :, thin[c]] = b.t3s[rows(z, TR), thin[c]]
+
+        def grads_out(c):
+            width = sizes[c] // G
+            got(S.t3 + marks[c])
+            total = b.t3r[0, :, thin[c]].astype(F32)
+            for k in range(1, Z):
+                total = total + b.t3r[k, :, thin[c]].astype(F32)
+            total = total * (1.0 / math.sqrt(n * TOK))
+            for g in range(G):
+                at = pl.ds(begins[c] + g * width, width)
+                gup_ref[:, at] = total[2 * g * E : (2 * g + 1) * E, :]
+                gdn_ref[:, at] = total[(2 * g + 1) * E : (2 * g + 2) * E, :]
 
         for c in range(2):
 
-            @pl.loop(c * (FH // wide), (c + 1) * (FH // wide))
+            @pl.loop(begins[c] // wide, (begins[c] + sizes[c]) // wide)
             def _(k):
                 at = cols(k, wide)
                 pre = dot(b.mlp[...], b.upw[:, at])
@@ -622,6 +656,11 @@
             ring_start(b.gu, x, X, at_x, S.gu, c)
             ring_start(b.gd, y, Y, at_y, S.gd, c)
 
+        def grads_rest(c):
+            ring_rest(b.gu, x, X, at_x, S.gu, c)
+            ring_rest(b.gd, y, Y, at_y, S.gd, c)
+
+        grads_rest(0)
         hidden = b.gd.at[rows(y, TOK)]
         d_pre = b.gu.at[rows(x, TOK)]
         for k in range(D // 256):
@@ -639,18 +678,7 @@
                 mu_all,
                 mu_all,
             )
-        for k in range(1, Y):
-            to = lax.rem(y + k, Y)
-            send(
-                b.cdn.at[rows(to, QY)],
-                b.md.at[:, cols(y, TOK)],
-                S.md,
-                at_y(to),
-                md_all,
-                md_all,
-            )
         b.mu[:, cols(x, TOK)] = b.mup[rows(x, QX), :]
-        b.md[:, cols(y, TOK)] = b.cdn[rows(y, QY), :]
 
         got(S.back)
         d_n2 = (b.back[...] + b.back_r[...]) * mlp_gain
@@ -665,29 +693,28 @@
 
         grads_relay(0)
         conv_plane(1, "b")
+        grads_rest(1)
         grads_relay(1)
-
+        grads_local(0)
+
+        conv_work(1, "b", -1.0)
+
+        grads_local(1)
+        grads_pass(0)
+        conv_return(1, "b")
+        grads_pass(1)
+        grads_z(0)
         for k in range(D // 256):
             at = slice(k * 256, (k + 1) * 256)
             b.down[:, at] = dot_t(hidden[...], b.dnw[at, :])
         send(b.down.at[:, cols(1 - h, C)], b.down_r, S.down, other)
-        got(S.down)
-        out_ref[...] = (b.resid[:, own] + b.down[:, own] + b.down_r[...]).astype(BF16)
-        conv_work(1, "b", -1.0)
-
-        grads_local(0)
-        conv_return(1, "b")
-        grads_local(1)
-        grads_pass(0)
+        grads_z(1)
         d_signal = conv_in(1, "b")
         b.dshort[0, 0:TOK, :] = d_signal * b.shorted[1]
         b.dshort[1, 0:TOK, :] = d_signal * b.shorted[0]
         for j in range(3):
             b.edge[j] = b.dshort[j, 0:8, :]
         send(b.edge, b.dshort.at[:, TOK:, :], S.edge, (prv, h))
-        grads_z(0)
-        grads_pass(1)
-
         MAIN = TOK - HALO
         for j in range(3):
             value = b.dshort[j, 0:TOK, :]
@@ -700,6 +727,8 @@
             else:
                 b.inp[0:MAIN, :] += part
         send(b.inp.at[0:MAIN], b.inp_r.at[0:MAIN], S.inp, other)
+        got(S.down)
+        out_ref[...] = (b.resid[:, own] + b.down[:, own] + b.down_r[...]).astype(BF16)
         got(S.edge)
         last = s == n - 1
         row = lax.broadcasted_iota(jnp.int32, (HALO + 8, 1), 0)
@@ -715,7 +744,6 @@
             else:
                 b.inp[MAIN:, :] += part
         send(b.inp.at[MAIN:], b.inp_r.at[MAIN:], S.inq, other)
-        grads_z(1)
         got(S.inq)
         got(S.inp)
         d_n1 = (b.inp[...] + b.inp_r[...]) * norm_gain
@@ -726,14 +754,8 @@
         b.gtok[...] = b.dres[...] + scale_in * (d_n1 - normed * inner)
         gtok_ref[...] = b.gtok[:, own].astype(BF16)
 
-        got(S.t3 + "a")
-        got(S.t3 + "b")
-        total = b.t3r[0].astype(F32)
-        for k in range(1, Z):
-            total = total + b.t3r[k].astype(F32)
-        total = total * (1.0 / math.sqrt(n * TOK))
-        gup_ref[...] = total[0:E, :]
-        gdn_ref[...] = total[EP : EP + E, :]
+        grads_out(0)
+        grads_out(1)
 
         for name in list(leaving):
             sent(name)

time: 85.5 us -> 81.3 us (0.951)
  the two profiles are of different devices: /device:TPU:1 before, /device:TPU:31 now
where the time goes in v2:
time: 81.3 us; the launch traced here: 81.2 us
  Pallas kernels  80.6 us (99%)
    pallas_call x1, Pallas kernels, local(): pl.pallas_call(kernel, out_shape=(jax.ShapeDtypeStruct((rows, chans), BF1...  78.9 us
    pallas_call x1, Pallas kernels, local(): pl.pallas_call(hand_over, out_shape=tuple((jax.ShapeDtypeStruct(part.shap...  1.66 us

profile of v2, /device:TPU:31, one launch (start us, length us, event | category | flops | bytes accessed | tf_op | source)
XLA Modules:
  0.0 81.2 jit_solution(15125433440816064795)
XLA Ops:
  0.6 78.9 %shard_map.228 = (bf16[128,384]{1,0:T(8,128)(2,1)}, bf16[128,384]{1,0:T(8,128)(2,1)}, f32[6,1536]{1,0:T(8,128)}, f32[6,1536]{1,0:T(8,128)}) custom-call(bf16[128,384]{1,0:T(8,128)(2,1)} %refs_0_.1, f32[384]{0:T(512)} %refs_1_.1, bf16[3,768,384]{2,1,0:T(8,128)(2,1)} %refs_2_.1, f32[3,3,384]{2,1,0:T(4,128)} %refs_3_.1, f32[2,128,384]{2,1,0:T(8,128)} %refs_4_.1, ...), custom_call_target="tpu_custom_call" | custom-call | tf_op jit(solution)/shard_map/pallas_call | solution.py:785
  79.6 1.7 %shard_map.229 = (bf16[128,384]{1,0:T(8,128)(2,1)}, bf16[128,384]{1,0:T(8,128)(2,1)}, f32[6,1536]{1,0:T(8,128)}, f32[6,1536]{1,0:T(8,128)}) custom-call(bf16[128,384]{1,0:T(8,128)(2,1)} %get-tuple-element.8.refs_0_, bf16[128,384]{1,0:T(8,128)(2,1)} %get-tuple-element.9.refs_1_, f32[6,1536]{1,0:T(8,128)} %get-tuple-element.10.refs_2_, ...), custom_call_target="tpu_custom_call" | custom-call | tf_op jit(solution)/shard_map/pallas_call | solution.py:817
